TPU v7x, 32 devices: a whole 2x2x4 slice. The times are simulated.
32 devices in a mesh: tm: 16 (over z, y, x), head: 2 (over core).
Axes of the slice: x: 2, y: 2, z: 4, core: 2. Of those that a mesh axis runs over, the one named last changes fastest.
Arguments:
- queries: bfloat16 [2048, 4096], P('tm', 'head'), may hold values from -6 to 6
- keys: bfloat16 [2048, 4096], P('tm', 'head'), may hold values from -6 to 6
- values: bfloat16 [2048, 4096], P('tm', 'head'), may hold values from -6 to 6
- log_decay: float32 [32, 2048], P('head', 'tm'), may hold values from -1 to 0
- agent_ids: int32 [2048], P('tm'), may hold values from 0 to 127
- norm_gain: float32 [4096], P('head'), may hold values from 0.1 to 1.9
- out_grad: bfloat16 [2048, 4096], P('tm', 'head'), may hold values from -6 to 6
Outputs:
- result: bfloat16 [2048, 4096], P('tm', 'head')
- query_grad: bfloat16 [2048, 4096], P('tm', 'head')
- key_grad: bfloat16 [2048, 4096], P('tm', 'head')
- value_grad: bfloat16 [2048, 4096], P('tm', 'head')
- decay_grad: float32 [32, 2048], P('head', 'tm')
- gain_grad: float32 [4096], P('head')
All inputs are finite; a program needn't handle non-finite values.
Results may differ from a plain program's by a relative error of at most 0.001.
Values sent between devices are 32-bit elements; how exact they have to be, the bound alone decides.
A program may use at most 128 MiB of HBM per device.

v0:
```python
import jax
import jax.numpy as jnp
from jax import lax
from jax.sharding import PartitionSpec as P

DK = 128
GROUP = 128
TEAM = 16
WIDTH = 4096


EPS = 1e-06
HIGH = lax.Precision.HIGHEST


def passed_along(value, axis, steps):
    count = lax.axis_size(axis)
    leading, last = (max(0, -steps), min(count, count - steps))
    return lax.ppermute(value, axis, [(source, source + steps) for source in range(leading, last)])


def group_pass(scaled, key_rows, value_rows, decays, teams):
    length, heads, depth = scaled.shape
    blocks = length // GROUP
    query_blocks = scaled.reshape(blocks, GROUP, heads, depth)
    key_blocks = key_rows.reshape(blocks, GROUP, heads, depth)
    value_blocks = value_rows.reshape(blocks, GROUP, heads, depth)
    decay_blocks = decays.reshape(heads, blocks, GROUP).transpose(1, 0, 2)
    team_blocks = teams.reshape(blocks, GROUP)
    places = jnp.arange(GROUP)
    causal = places[:, None] >= places[None, :]

    def advance(state, inputs):
        query_block, key_block, value_block, decay_block, team_block = inputs
        cumulative = jnp.cumsum(decay_block, axis=1)
        visible = (causal & (team_block[:, None] == team_block[None, :]))[None]
        spread = cumulative[:, :, None] - cumulative[:, None, :]
        weights = jnp.where(visible, jnp.exp(jnp.where(visible, spread, 0.0)), 0.0)
        scores = jnp.einsum("thd,shd->hts", query_block, key_block, precision=HIGH) * weights
        output = jnp.einsum("hts,she->the", scores, value_block, precision=HIGH)
        carried = jnp.einsum("thd,hde->the", query_block, state, precision=HIGH)
        output = output + jnp.exp(cumulative).T[:, :, None] * carried
        tail = jnp.exp(cumulative[:, -1:] - cumulative)
        fresh = jnp.einsum(
            "shd,she->hde", key_block * tail.T[:, :, None], value_block, precision=HIGH
        )
        state = jnp.exp(cumulative[:, -1])[:, None, None] * state + fresh
        return (state, output)

    start = jnp.zeros((heads, depth, depth), jnp.float32)
    final, outputs = lax.scan(
        advance, start, (query_blocks, key_blocks, value_blocks, decay_blocks, team_blocks)
    )
    return (outputs.reshape(length, heads, depth), final)


def combine(earlier, later):
    return (earlier[0] * later[0], later[0][:, None, None] * earlier[1] + later[1])


def body(queries, keys, values, log_decay, agent_ids, norm_gain, out_grad):
    length = queries.shape[0]
    heads_here = queries.shape[1] // DK
    factor_q = DK ** (-0.5)
    scaled = queries.astype(jnp.float32).reshape(length, heads_here, DK) * factor_q
    key_rows = keys.astype(jnp.float32).reshape(length, heads_here, DK)
    value_rows = values.astype(jnp.float32).reshape(length, heads_here, DK)
    teams = agent_ids // TEAM

    def local_pass(query_in, key_in, value_in, decays):
        return group_pass(query_in, key_in, value_in, decays, teams)

    (local_out, local_end), pullback = jax.vjp(local_pass, scaled, key_rows, value_rows, log_decay)
    cumulative = jnp.cumsum(log_decay, axis=1)
    factor = jnp.exp(cumulative[:, -1])
    count = lax.axis_size("tm")
    running = (factor, local_end)
    for level in range((count - 1).bit_length()):
        earlier = passed_along((running[0], running[1]), "tm", 1 << level)
        running = combine(earlier, running)
    state_in = passed_along(running[1], "tm", 1)
    inter_term = jnp.einsum("thd,hde->the", scaled, state_in, precision=HIGH)
    weights = jnp.exp(cumulative).T[:, :, None]
    output = local_out + weights * inter_term
    flat = output.reshape(length, heads_here * DK)
    grad_rows = out_grad.astype(jnp.float32)
    scaled_grad = grad_rows * norm_gain
    square_part = jnp.sum(flat * flat, axis=1)
    square_sum = lax.psum(square_part, "head")
    rms_value = jnp.sqrt(square_sum / WIDTH + EPS)
    normed = flat / rms_value[:, None]
    result = (normed * norm_gain).astype(jnp.bfloat16)
    inner_sum = lax.psum(jnp.sum(scaled_grad * flat, axis=1), "head")
    gain_grad = lax.psum(jnp.sum(grad_rows * normed, axis=0), "tm")
    flat_grad = (
        scaled_grad / rms_value[:, None] - flat * (inner_sum / (WIDTH * rms_value**3))[:, None]
    )
    out_adjoint = flat_grad.reshape(length, heads_here, DK)
    weighted = out_adjoint * weights
    own_adjoint = jnp.einsum("thd,the->hde", scaled, weighted, precision=HIGH)
    running = (factor, own_adjoint)
    for level in range((count - 1).bit_length()):
        later_side = passed_along((running[0], running[1]), "tm", -(1 << level))
        running = combine(later_side, running)
    end_adjoint = passed_along(running[1], "tm", -1)
    query_part, key_part, value_part, decay_part = pullback((out_adjoint, end_adjoint))
    query_total = query_part + weights * jnp.einsum(
        "the,hde->thd", out_adjoint, state_in, precision=HIGH
    )
    reach = jnp.sum(weights * inter_term * out_adjoint, axis=2).T
    reach_back = jnp.flip(jnp.cumsum(jnp.flip(reach, 1), axis=1), 1)
    through_end = factor * jnp.sum(end_adjoint * state_in, axis=(1, 2))
    decay_grad = decay_part + reach_back + through_end[:, None]
    query_grad = (query_total * factor_q).reshape(length, heads_here * DK).astype(jnp.bfloat16)
    key_grad = key_part.reshape(length, heads_here * DK).astype(jnp.bfloat16)
    value_grad = value_part.reshape(length, heads_here * DK).astype(jnp.bfloat16)
    return (result, query_grad, key_grad, value_grad, decay_grad, gain_grad)


def solution(mesh):
    placed = (
        P("tm", "head"),
        P("tm", "head"),
        P("tm", "head"),
        P("head", "tm"),
        P("tm"),
        P("head"),
        P("tm", "head"),
    )
    return jax.shard_map(
        body,
        mesh=mesh,
        in_specs=placed,
        out_specs=(
            P("tm", "head"),
            P("tm", "head"),
            P("tm", "head"),
            P("tm", "head"),
            P("head", "tm"),
            P("head"),
        ),
        check_vma=False,
    )
```

profile of v0, /device:TPU:0, one launch (start us, length us, event | category | flops | bytes accessed | tf_op | source)
XLA Modules:
  0.0 393.2 jit_solution(13272700838115090436)
XLA Ops:
  1.9 1.3 collective-permute-start.8
  3.2 5.5 %collective-permute-start = (f32[16]{0:T(128)S(1)}, f32[16]{0:T(128)S(1)}, u32[]{:S(2)}, u32[]{:S(2)}) collective-permute-start(f32[16]{0:T(128)S(1)} %exp.100), channel_id=1, source_target_pairs={{0,2},{2,4},{4,6},{6,8},{8,10},{10,12},{12,14},{14,16},{16,18},{18... | collective-permute-start | bytes 200 | tf_op jit(solution)/shard_map/ppermute | solution.py:19
  8.7 1.3 copy.41
  10.8 4.9 %collective-permute-start.3 = (f32[16,128,128]{2,1,0:T(8,128)S(1)}, f32[16,128,128]{2,1,0:T(8,128)S(1)}, u32[]{:S(2)}, u32[]{:S(2)}) collective-permute-start(f32[16,128,128]{2,1,0:T(8,128)S(1)} %convolution_add_fusion.2), channel_id=1, source_target_pairs={{0,2},{2,4},{4,6},{6,8},{8,10},{10,12},{12,14},{14,16},{16,18},{18... | collective-permute-start | bytes 3145736 | tf_op jit(solution)/shard_map/ppermute | solution.py:19
  15.7 21.8 %collective-permute-done.3 = f32[16,128,128]{2,1,0:T(8,128)S(1)} collective-permute-done((f32[16,128,128]{2,1,0:T(8,128)S(1)}, f32[16,128,128]{2,1,0:T(8,128)S(1)}, u32[]{:S(2)}, u32[]{:S(2)}) %collective-permute-start.3) | collective-permute-done | bytes 1048608 | tf_op jit(solution)/shard_map/ppermute | solution.py:19
  37.6 6.0 %collective-permute-start.4 = (f32[16,128,128]{2,1,0:T(8,128)S(1)}, f32[16,128,128]{2,1,0:T(8,128)S(1)}, u32[]{:S(2)}, u32[]{:S(2)}) collective-permute-start(f32[16,128,128]{2,1,0:T(8,128)S(1)} %multiply_add_fusion.7), channel_id=1, source_target_pairs={{0,4},{2,6},{4,8},{6,10},{8,12},{10,14},{12,16},{14,18},{16,20},{1... | collective-permute-start | bytes 3145736 | tf_op jit(solution)/shard_map/ppermute | solution.py:19
  43.6 20.0 %collective-permute-done.4 = f32[16,128,128]{2,1,0:T(8,128)S(1)} collective-permute-done((f32[16,128,128]{2,1,0:T(8,128)S(1)}, f32[16,128,128]{2,1,0:T(8,128)S(1)}, u32[]{:S(2)}, u32[]{:S(2)}) %collective-permute-start.4) | collective-permute-done | bytes 1048608 | tf_op jit(solution)/shard_map/ppermute | solution.py:19
  63.8 8.1 %collective-permute-start.5 = (f32[16,128,128]{2,1,0:T(8,128)S(1)}, f32[16,128,128]{2,1,0:T(8,128)S(1)}, u32[]{:S(2)}, u32[]{:S(2)}) collective-permute-start(f32[16,128,128]{2,1,0:T(8,128)S(1)} %multiply_add_fusion.6), channel_id=1, source_target_pairs={{0,8},{2,10},{4,12},{6,14},{8,16},{10,18},{12,20},{14,22},{16,24},... | collective-permute-start | bytes 3145736 | tf_op jit(solution)/shard_map/ppermute | solution.py:19
  71.9 1.6 collective-permute-start.1
  74.8 16.2 %collective-permute-done.5 = f32[16,128,128]{2,1,0:T(8,128)S(1)} collective-permute-done((f32[16,128,128]{2,1,0:T(8,128)S(1)}, f32[16,128,128]{2,1,0:T(8,128)S(1)}, u32[]{:S(2)}, u32[]{:S(2)}) %collective-permute-start.5) | collective-permute-done | bytes 1048608 | tf_op jit(solution)/shard_map/ppermute | solution.py:19
  91.1 5.5 %collective-permute-start.6 = (f32[16,128,128]{2,1,0:T(8,128)S(1)}, f32[16,128,128]{2,1,0:T(8,128)S(1)}, u32[]{:S(2)}, u32[]{:S(2)}) collective-permute-start(f32[16,128,128]{2,1,0:T(8,128)S(1)} %multiply_add_fusion.5), channel_id=1, source_target_pairs={{0,16},{2,18},{4,20},{6,22},{8,24},{10,26},{12,28},{14,30},{1,17},... | collective-permute-start | bytes 3145736 | tf_op jit(solution)/shard_map/ppermute | solution.py:19
  96.6 3.5 collective-permute-start.2
  100.1 14.7 %collective-permute-done.2 = f32[16]{0:T(128)S(1)} collective-permute-done((f32[16]{0:T(128)S(1)}, f32[16]{0:T(128)S(1)}, u32[]{:S(2)}, u32[]{:S(2)}) %collective-permute-start.2) | collective-permute-done | bytes 96 | tf_op jit(solution)/shard_map/ppermute | solution.py:19
  116.0 1.4 collective-permute-start.7
  118.6 1.6 copy.77
  122.5 12.7 %collective-permute-done.7 = f32[16,128,128]{2,1,0:T(8,128)S(1)} collective-permute-done((f32[16,128,128]{2,1,0:T(8,128)}, f32[16,128,128]{2,1,0:T(8,128)S(1)}, u32[]{:S(2)}, u32[]{:S(2)}) %collective-permute-start.7) | collective-permute-done | bytes 1048608 | tf_op jit(solution)/shard_map/ppermute | solution.py:19
  135.2 1.8 fusion.3
  137.1 2.6 multiply_reduce_fusion.4
  139.7 2.4 psum.21
  142.1 1.6 copy.50
  143.7 1.4 fusion.14
  145.1 2.5 psum.22
  147.6 2.5 fusion.11
  150.1 1.5 copy.53
  151.7 2.3 fusion.20
  154.0 1.3 collective-permute-start.11
  155.3 26.5 %collective-permute-done.11 = f32[16,128,128]{2,1,0:T(8,128)S(1)} collective-permute-done((f32[16,128,128]{2,1,0:T(8,128)S(1)}, f32[16,128,128]{2,1,0:T(8,128)S(1)}, u32[]{:S(2)}, u32[]{:S(2)}) %collective-permute-start.11) | collective-permute-done | bytes 1048608 | tf_op jit(solution)/shard_map/ppermute | solution.py:19
  181.9 1.5 collective-permute-start.12
  183.4 53.4 %collective-permute-done.12 = f32[16,128,128]{2,1,0:T(8,128)S(1)} collective-permute-done((f32[16,128,128]{2,1,0:T(8,128)S(1)}, f32[16,128,128]{2,1,0:T(8,128)S(1)}, u32[]{:S(2)}, u32[]{:S(2)}) %collective-permute-start.12) | collective-permute-done | bytes 1048608 | tf_op jit(solution)/shard_map/ppermute | solution.py:19
  237.0 1.3 collective-permute-start.13
  238.3 1.3 collective-permute-start.9
  239.6 6.2 %collective-permute-done.9 = f32[16]{0:T(128)S(1)} collective-permute-done((f32[16]{0:T(128)S(1)}, f32[16]{0:T(128)S(1)}, u32[]{:S(2)}, u32[]{:S(2)}) %collective-permute-start.9) | collective-permute-done | bytes 96 | tf_op jit(solution)/shard_map/ppermute | solution.py:19
  245.9 19.2 %collective-permute-done.13 = f32[16,128,128]{2,1,0:T(8,128)S(1)} collective-permute-done((f32[16,128,128]{2,1,0:T(8,128)S(1)}, f32[16,128,128]{2,1,0:T(8,128)S(1)}, u32[]{:S(2)}, u32[]{:S(2)}) %collective-permute-start.13) | collective-permute-done | bytes 1048608 | tf_op jit(solution)/shard_map/ppermute | solution.py:19
  265.2 1.3 collective-permute-start.14
  266.5 1.3 collective-permute-start.10
  267.8 4.3 %collective-permute-done.10 = f32[16]{0:T(128)S(1)} collective-permute-done((f32[16]{0:T(128)S(1)}, f32[16]{0:T(128)S(1)}, u32[]{:S(2)}, u32[]{:S(2)}) %collective-permute-start.10) | collective-permute-done | bytes 96 | tf_op jit(solution)/shard_map/ppermute | solution.py:19
  272.1 2.1 fusion.15
  274.2 2.3 fusion.62
  276.5 36.8 %collective-permute-done.14 = f32[16,128,128]{2,1,0:T(8,128)S(1)} collective-permute-done((f32[16,128,128]{2,1,0:T(8,128)S(1)}, f32[16,128,128]{2,1,0:T(8,128)S(1)}, u32[]{:S(2)}, u32[]{:S(2)}) %collective-permute-start.14) | collective-permute-done | bytes 1048608 | tf_op jit(solution)/shard_map/ppermute | solution.py:19
  316.6 3.1 fusion.2
  319.7 2.1 fusion.8
  321.7 2.0 copy.66
  323.8 52.0 %psum.23 = f32[2048]{0:T(1024)} all-reduce(f32[2048]{0:T(1024)S(1)} %get-tuple-element.252), channel_id=1, replica_groups=mesh['tm'=16,'head'=2] {'tm'}, use_global_device_ids=true, to_apply=%region_16.17 | all-reduce | flops 2048 | bytes 16384 | tf_op jit(solution)/shard_map/psum | solution.py:94
  375.8 3.6 fusion.23
  379.4 2.5 fusion.13
  382.0 1.5 add_convert_fusion
  384.9 3.0 fusion.7
  389.4 1.5 multiply_reduce_fusion
  (75 shorter events, 17.3 us)
Async XLA Ops:
  0.6 9.5 %copy-start = (bf16[128,2048]{1,0:T(8,128)(2,1)S(1)}, bf16[128,2048]{1,0:T(8,128)(2,1)}, u32[]{:S(2)}) copy-start(bf16[128,2048]{1,0:T(8,128)(2,1)} %param.9) | copy-start | bytes 1572868
  1.9 8.2 %collective-permute-start.8 = (f32[16]{0:T(128)S(1)}, f32[16]{0:T(128)S(1)}, u32[]{:S(2)}, u32[]{:S(2)}) collective-permute-start(f32[16]{0:T(128)S(1)} %exp.100), channel_id=1, source_target_pairs={{2,0},{4,2},{6,4},{8,6},{10,8},{12,10},{14,12},{16,14},{18,16},{20... | collective-permute-start | bytes 200 | tf_op jit(solution)/shard_map/ppermute | solution.py:19
  3.2 6.9 %collective-permute-start = (f32[16]{0:T(128)S(1)}, f32[16]{0:T(128)S(1)}, u32[]{:S(2)}, u32[]{:S(2)}) collective-permute-start(f32[16]{0:T(128)S(1)} %exp.100), channel_id=1, source_target_pairs={{0,2},{2,4},{4,6},{6,8},{8,10},{10,12},{12,14},{14,16},{16,18},{18... | collective-permute-start | bytes 200 | tf_op jit(solution)/shard_map/ppermute | solution.py:19
  10.8 26.7 %collective-permute-start.3 = (f32[16,128,128]{2,1,0:T(8,128)S(1)}, f32[16,128,128]{2,1,0:T(8,128)S(1)}, u32[]{:S(2)}, u32[]{:S(2)}) collective-permute-start(f32[16,128,128]{2,1,0:T(8,128)S(1)} %convolution_add_fusion.2), channel_id=1, source_target_pairs={{0,2},{2,4},{4,6},{6,8},{8,10},{10,12},{12,14},{14,16},{16,18},{18... | collective-permute-start | bytes 3145736 | tf_op jit(solution)/shard_map/ppermute | solution.py:19
  37.6 26.0 %collective-permute-start.4 = (f32[16,128,128]{2,1,0:T(8,128)S(1)}, f32[16,128,128]{2,1,0:T(8,128)S(1)}, u32[]{:S(2)}, u32[]{:S(2)}) collective-permute-start(f32[16,128,128]{2,1,0:T(8,128)S(1)} %multiply_add_fusion.7), channel_id=1, source_target_pairs={{0,4},{2,6},{4,8},{6,10},{8,12},{10,14},{12,16},{14,18},{16,20},{1... | collective-permute-start | bytes 3145736 | tf_op jit(solution)/shard_map/ppermute | solution.py:19
  63.8 27.2 %collective-permute-start.5 = (f32[16,128,128]{2,1,0:T(8,128)S(1)}, f32[16,128,128]{2,1,0:T(8,128)S(1)}, u32[]{:S(2)}, u32[]{:S(2)}) collective-permute-start(f32[16,128,128]{2,1,0:T(8,128)S(1)} %multiply_add_fusion.6), channel_id=1, source_target_pairs={{0,8},{2,10},{4,12},{6,14},{8,16},{10,18},{12,20},{14,22},{16,24},... | collective-permute-start | bytes 3145736 | tf_op jit(solution)/shard_map/ppermute | solution.py:19
  71.9 2.8 collective-permute-start.1
  91.1 23.7 %collective-permute-start.6 = (f32[16,128,128]{2,1,0:T(8,128)S(1)}, f32[16,128,128]{2,1,0:T(8,128)S(1)}, u32[]{:S(2)}, u32[]{:S(2)}) collective-permute-start(f32[16,128,128]{2,1,0:T(8,128)S(1)} %multiply_add_fusion.5), channel_id=1, source_target_pairs={{0,16},{2,18},{4,20},{6,22},{8,24},{10,26},{12,28},{14,30},{1,17},... | collective-permute-start | bytes 3145736 | tf_op jit(solution)/shard_map/ppermute | solution.py:19
  96.6 18.2 %collective-permute-start.2 = (f32[16]{0:T(128)S(1)}, f32[16]{0:T(128)S(1)}, u32[]{:S(2)}, u32[]{:S(2)}) collective-permute-start(f32[16]{0:T(128)S(1)} %mul.308), channel_id=1, source_target_pairs={{0,8},{2,10},{4,12},{6,14},{8,16},{10,18},{12,20},{14,22},{16,24},... | collective-permute-start | bytes 200 | tf_op jit(solution)/shard_map/ppermute | solution.py:19
  114.8 2.6 copy-start.12
  116.0 19.2 %collective-permute-start.7 = (f32[16,128,128]{2,1,0:T(8,128)}, f32[16,128,128]{2,1,0:T(8,128)S(1)}, u32[]{:S(2)}, u32[]{:S(2)}) collective-permute-start(f32[16,128,128]{2,1,0:T(8,128)} %multiply_add_fusion.4), channel_id=1, source_target_pairs={{0,2},{2,4},{4,6},{6,8},{8,10},{10,12},{12,14},{14,16},{16,18},{18... | collective-permute-start | bytes 3145736 | tf_op jit(solution)/shard_map/ppermute | solution.py:19
  118.6 1.6 copy-start.14
  121.5 15.6 %copy-start.5 = (f32[128,16,128]{0,2,1:T(8,128)}, f32[128,16,128]{0,2,1:T(8,128)S(1)}, u32[]{:S(2)}) copy-start(f32[128,16,128]{0,2,1:T(8,128)S(1)} %convolution_bitcast_fusion.3) | copy-start | bytes 3145732
  122.5 14.6 %copy-start.3 = (f32[16,128,128]{2,1,0:T(8,128)}, f32[16,128,128]{2,1,0:T(8,128)S(1)}, u32[]{:S(2)}) copy-start(f32[16,128,128]{2,1,0:T(8,128)S(1)} %fusion.78) | copy-start | bytes 3145732
  135.2 1.9 copy-start.7
  137.1 2.6 copy-start.1
  142.1 1.6 copy-start.13
  154.0 27.8 %collective-permute-start.11 = (f32[16,128,128]{2,1,0:T(8,128)S(1)}, f32[16,128,128]{2,1,0:T(8,128)S(1)}, u32[]{:S(2)}, u32[]{:S(2)}) collective-permute-start(f32[16,128,128]{2,1,0:T(8,128)S(1)} %fusion.20), channel_id=1, source_target_pairs={{2,0},{4,2},{6,4},{8,6},{10,8},{12,10},{14,12},{16,14},{18,16},{20... | collective-permute-start | bytes 3145736 | tf_op jit(solution)/shard_map/ppermute | solution.py:19
  181.9 54.9 %collective-permute-start.12 = (f32[16,128,128]{2,1,0:T(8,128)S(1)}, f32[16,128,128]{2,1,0:T(8,128)S(1)}, u32[]{:S(2)}, u32[]{:S(2)}) collective-permute-start(f32[16,128,128]{2,1,0:T(8,128)S(1)} %multiply_add_fusion.3), channel_id=1, source_target_pairs={{4,0},{6,2},{8,4},{10,6},{12,8},{14,10},{16,12},{18,14},{20,16},{2... | collective-permute-start | bytes 3145736 | tf_op jit(solution)/shard_map/ppermute | solution.py:19
  237.0 28.1 %collective-permute-start.13 = (f32[16,128,128]{2,1,0:T(8,128)S(1)}, f32[16,128,128]{2,1,0:T(8,128)S(1)}, u32[]{:S(2)}, u32[]{:S(2)}) collective-permute-start(f32[16,128,128]{2,1,0:T(8,128)S(1)} %multiply_add_fusion.2), channel_id=1, source_target_pairs={{8,0},{10,2},{12,4},{14,6},{16,8},{18,10},{20,12},{22,14},{24,16},... | collective-permute-start | bytes 3145736 | tf_op jit(solution)/shard_map/ppermute | solution.py:19
  238.3 7.5 %collective-permute-start.9 = (f32[16]{0:T(128)S(1)}, f32[16]{0:T(128)S(1)}, u32[]{:S(2)}, u32[]{:S(2)}) collective-permute-start(f32[16]{0:T(128)S(1)} %get-tuple-element.264), channel_id=1, source_target_pairs={{4,0},{6,2},{8,4},{10,6},{12,8},{14,10},{16,12},{18,14},{20,16},{2... | collective-permute-start | bytes 200 | tf_op jit(solution)/shard_map/ppermute | solution.py:19
  265.2 48.1 %collective-permute-start.14 = (f32[16,128,128]{2,1,0:T(8,128)S(1)}, f32[16,128,128]{2,1,0:T(8,128)S(1)}, u32[]{:S(2)}, u32[]{:S(2)}) collective-permute-start(f32[16,128,128]{2,1,0:T(8,128)S(1)} %multiply_add_fusion.1), channel_id=1, source_target_pairs={{16,0},{18,2},{20,4},{22,6},{24,8},{26,10},{28,12},{30,14},{17,1},... | collective-permute-start | bytes 3145736 | tf_op jit(solution)/shard_map/ppermute | solution.py:19
  266.5 5.6 %collective-permute-start.10 = (f32[16]{0:T(128)S(1)}, f32[16]{0:T(128)S(1)}, u32[]{:S(2)}, u32[]{:S(2)}) collective-permute-start(f32[16]{0:T(128)S(1)} %mul.336), channel_id=1, source_target_pairs={{8,0},{10,2},{12,4},{14,6},{16,8},{18,10},{20,12},{22,14},{24,16},... | collective-permute-start | bytes 200 | tf_op jit(solution)/shard_map/ppermute | solution.py:19
  272.1 2.1 copy-start.4
  276.5 39.3 %copy-start.2 = (f32[128,16,128]{0,2,1:T(8,128)S(1)}, f32[128,16,128]{0,2,1:T(8,128)}, u32[]{:S(2)}) copy-start(f32[128,16,128]{0,2,1:T(8,128)} %copy-done.1) | copy-start | bytes 3145732
  276.5 39.3 %copy-start.6 = (f32[128,16,128]{0,2,1:T(8,128)S(1)}, f32[128,16,128]{0,2,1:T(8,128)}, u32[]{:S(2)}) copy-start(f32[128,16,128]{0,2,1:T(8,128)} %copy-done.5) | copy-start | bytes 3145732
  314.5 64.9 %collective-permute-start.15 = (f32[16,128,128]{2,1,0:T(8,128)}, f32[16,128,128]{2,1,0:T(8,128)}, u32[]{:S(2)}, u32[]{:S(2)}) collective-permute-start(f32[16,128,128]{2,1,0:T(8,128)} %multiply_add_fusion), channel_id=1, source_target_pairs={{2,0},{4,2},{6,4},{8,6},{10,8},{12,10},{14,12},{16,14},{18,16},{20... | collective-permute-start | bytes 3145736 | tf_op jit(solution)/shard_map/ppermute | solution.py:19
  316.6 3.1 copy-start.8
  379.4 2.6 copy-start.10
  383.5 1.4 copy-start.11
  388.0 1.4 copy-start.9
where the time goes:
time: 394 us; the launch traced here: 393 us
  waiting for transfers between devices  233 us (59%)
  blocking collectives  56.9 us (14%)
  starting transfers between devices  46.9 us (12%)
  matrix products  29.9 us (8%)
  other arithmetic  14.1 us (4%)
  local copies, waits for them, and re-layouts  11.2 us (3%)
    ppermute x16, waiting for transfers between devices, passed_along(): lax.ppermute(value, axis, [(source, source + steps) for source in range(l...  233 us
    psum x1, blocking collectives, body(): gain_grad = lax.psum(jnp.sum(grad_rows * normed, axis=0), 'tm')  52 us
    ppermute x16, starting transfers between devices, passed_along(): lax.ppermute(value, axis, [(source, source + steps) for source in range(l...  46.9 us
    dot_general x3, matrix products, advance(): output = jnp.einsum('hts,she->the', scores, value_block, precision=HIGH)  8.48 us
  transfers between devices with their start and end apart: 16, of which 12 were waited for; matrix products, arithmetic and copies ran while one was open for 6% of the time, Pallas kernels for 0%

commit v1 on v0

v1 whole, which is shorter than its diff:
```python
import functools
import math

import jax
import jax.numpy as jnp
from jax import lax
from jax.experimental import pallas as pl
from jax.experimental.pallas import tpu as pltpu
from jax.sharding import PartitionSpec as P

DK = 128
TEAM = 16
EPS = 1e-06
UNROLL = 2
MESH = pl.DeviceIdType.MESH
F32, BF16 = jnp.float32, jnp.bfloat16
NN, NT, TN = ((1,), (0,)), ((1,), (1,)), ((0,), (0,))


def split(value, count=2):
    parts = []
    for _ in range(count):
        part = value.astype(BF16)
        parts.append(part)
        value = value - part.astype(F32)
    return tuple(parts)


def product(left, right, form):
    order = max(len(left), len(right))
    pairs = [(a, b) for i, a in enumerate(left) for j, b in enumerate(right) if i + j < order]
    lefts = jnp.concatenate([a for a, _ in pairs], axis=form[0][0])
    rights = jnp.concatenate([b for _, b in pairs], axis=form[1][0])
    return lax.dot_general(lefts, rights, (form, ((), ())), preferred_element_type=F32)


class Scan:
    def __init__(self, back, group, chain, share, refs, factors, sems, chain_sems):
        self.back, self.group, self.chain, self.share = back, group, chain, share
        self.own, self.dealt, self.came, self.gone, self.given, self.got = refs
        self.factors, self.sems, self.chain_sems = factors, sems, chain_sems
        me = lax.axis_index("tm")
        self.inner, self.outer = lax.rem(me, group), lax.div(me, group)
        self.sent = []

    def peer(self, step):
        return lax.rem(self.inner + step, self.group)

    def copy(self, source, target, send, receive, outer, inner):
        return pltpu.make_async_remote_copy(
            src_ref=source,
            dst_ref=target,
            send_sem=send,
            recv_sem=receive,
            device_id={"tm": outer * self.group + inner},
            device_id_type=MESH,
        )

    def deal_copy(self, step, chunk):
        peer = self.peer(step)
        sems = self.sems.at[0, :, step - 1, chunk]
        return self.copy(
            self.own.at[peer * self.share + chunk],
            self.dealt.at[self.inner, chunk],
            sems.at[0],
            sems.at[1],
            self.outer,
            peer,
        )

    def give_copy(self, step, chunk):
        peer = self.peer(step)
        sems = self.sems.at[1, :, step - 1, chunk]
        return self.copy(
            self.given.at[peer, chunk],
            self.got.at[self.inner * self.share + chunk],
            sems.at[0],
            sems.at[1],
            self.outer,
            peer,
        )

    def chain_copy(self, chunk):
        outer = self.outer + (-1 if self.back else 1)
        outer = lax.rem(outer + self.chain, self.chain)
        sems = self.chain_sems
        return self.copy(
            self.gone.at[chunk],
            self.came.at[chunk],
            sems.at[0, chunk],
            sems.at[1, chunk],
            outer,
            self.inner,
        )

    def first(self):
        return self.outer == (self.chain - 1 if self.back else 0)

    def last(self):
        return self.outer == (0 if self.back else self.chain - 1)

    def deal(self, chunk):
        for step in range(1, self.group):
            self.deal_copy(step, chunk).start()
        self.dealt[self.inner, chunk] = self.own[self.inner * self.share + chunk]

    def combine(self, chunk):
        for step in range(1, self.group):
            self.deal_copy(step, chunk).wait_recv()
        order = range(self.group)
        row = pl.ds(self.inner * self.share + chunk, 1)
        passed, through = None, []
        for place in reversed(order) if self.back else order:
            through.append((place, passed))
            factor = self.factors[place, row, :]
            term = self.dealt[place, chunk]
            if passed is None:
                total, passed = term, factor
                self.given[place, chunk] = jnp.zeros_like(term)
            else:
                self.given[place, chunk] = total
                total, passed = total * factor + term, passed * factor
        if self.chain > 1:

            @pl.when(self.first())
            def _():
                self.came[chunk] = jnp.zeros_like(total)

            @pl.when(jnp.logical_not(self.first()))
            def _():
                self.chain_copy(chunk).wait_recv()

            before = self.came[chunk]
            self.gone[chunk] = before * passed + total

            @pl.when(jnp.logical_not(self.last()))
            def _():
                self.chain_copy(chunk).start()

            for place, factor in through:
                added = before if factor is None else before * factor
                self.given[place, chunk] += added
        for step in range(1, self.group):
            self.give_copy(step, chunk).start()
        self.got[self.inner * self.share + chunk] = self.given[self.inner, chunk]

    def arrive(self, chunk):
        for step in range(1, self.group):
            self.give_copy(step, chunk).wait_recv()

    def finish(self):
        for chunk in range(self.share):
            for step in range(1, self.group):
                self.deal_copy(step, chunk).wait_send()
                self.give_copy(step, chunk).wait_send()
            if self.chain > 1:

                @pl.when(jnp.logical_not(self.last()))
                def _():
                    self.chain_copy(chunk).wait_send()


def kernel(
    group, chain, split_heads,
    q_ref, k_ref, v_ref, decay_ref, agent_ref, gain_ref, grad_ref,
    y_ref, q_grad_ref, k_grad_ref, v_grad_ref, decay_grad_ref, gain_grad_ref,
    sum_ref, total_ref, spread_ref, bias_ref, factor_ref, score_ref, weight_ref, out_ref, adjoint_ref,
    k_part_ref, v_part_ref, norm_ref, scale_ref, change_ref, gain_ref_in, gain_ref_out,
    end_ref, dealt_ref, came_ref, gone_ref, given_ref, state_ref,
    start_ref, dealt_back_ref, came_back_ref, gone_back_ref, given_back_ref, later_ref,
    scan_sems, chain_sems, factor_sems, norm_sems, gain_sems_in, gain_sems_out,
):
    length, width = q_ref.shape
    heads = width // DK
    share = heads // group
    scale = DK**-0.5
    full_width = width * split_heads
    me, side = lax.axis_index("tm"), lax.axis_index("head")
    inner, outer = lax.rem(me, group), lax.div(me, group)

    inner_peers = [outer * group + lax.rem(inner + step, group) for step in range(1, group)]
    outer_peers = [lax.rem(outer + step, chain) * group + inner for step in range(1, chain)]
    side_peers = [lax.rem(side + step, split_heads) for step in range(1, split_heads)]

    barrier = pltpu.get_barrier_semaphore()
    for peer in inner_peers + outer_peers:
        pl.semaphore_signal(barrier, inc=1, device_id={"tm": peer}, device_id_type=MESH)
    for peer in side_peers:
        pl.semaphore_signal(barrier, inc=1, device_id={"head": peer}, device_id_type=MESH)

    def to_peers(ref, place, peers, axis, sems):
        return [
            pltpu.make_async_remote_copy(
                src_ref=ref.at[place],
                dst_ref=ref.at[place],
                send_sem=sems.at[0, number],
                recv_sem=sems.at[1, number],
                device_id={axis: peer},
                device_id_type=MESH,
            )
            for number, peer in enumerate(peers)
        ]

    forward = Scan(
        False, group, chain, share,
        (end_ref, dealt_ref, came_ref, gone_ref, given_ref, state_ref),
        factor_ref, scan_sems.at[0], chain_sems.at[0],
    )
    backward = Scan(
        True, group, chain, share,
        (start_ref, dealt_back_ref, came_back_ref, gone_back_ref, given_back_ref, later_ref),
        factor_ref, scan_sems.at[1], chain_sems.at[1],
    )

    def columns(head):
        return pl.ds(pl.multiple_of(head * DK, DK), DK)

    def row(head):
        return pl.ds(head, 1)

    def each_head(chunk, work):
        def step(place, carry):
            work(place * share + chunk)
            return carry

        lax.fori_loop(0, group, step, None, unroll=UNROLL)

    rows_at = lax.broadcasted_iota(jnp.int32, (length, length), 0)
    lanes_at = lax.broadcasted_iota(jnp.int32, (length, length), 1)
    decays = split(decay_ref[...], 3)
    up_to = jnp.where(rows_at <= lanes_at, 1.0, 0.0).astype(BF16)
    sum_ref[...] = product(decays, (up_to,), NN)
    total_ref[...] = product(decays, (jnp.ones((length, DK), BF16),), NN)
    factor_ref[inner] = jnp.exp(total_ref[...])
    teams = jnp.broadcast_to(lax.div(agent_ref[...], TEAM).astype(F32), (length, length))
    visible = (rows_at >= lanes_at) & (teams == teams.T)
    bias_ref[...] = jnp.where(visible, 0.0, -1e30)

    def own_end(head):
        across = jnp.broadcast_to(sum_ref[row(head), :], (length, length))
        down = across.T
        spread_ref[head] = down
        tail = jnp.exp(total_ref[row(head), :] - down)
        keys = k_ref[:, columns(head)].astype(F32) * tail
        end_ref[head] = product(split(keys), (v_ref[:, columns(head)],), TN)

    each_head(0, own_end)
    pl.semaphore_wait(barrier, len(inner_peers) + len(outer_peers) + len(side_peers))
    factor_copies = to_peers(factor_ref, inner, inner_peers, "tm", factor_sems)
    for copy in factor_copies:
        copy.start()
    forward.deal(0)
    for chunk in range(1, share):
        each_head(chunk, own_end)
        forward.deal(chunk)

    def own_out(head):
        across = sum_ref[row(head), :]
        weight = jnp.exp(spread_ref[head] - across + bias_ref[...])
        weight_ref[head] = weight
        score = product((q_ref[:, columns(head)],), (k_ref[:, columns(head)],), NT) * weight * scale
        score_ref[head] = score
        out_ref[head] = product(split(score), (v_ref[:, columns(head)],), NN)

    for copy in factor_copies:
        copy.wait_recv()
    for chunk in range(share):
        each_head(chunk, own_out)
        forward.combine(chunk)

    norm_ref[side] = jnp.zeros_like(norm_ref[side])

    def whole_out(head):
        reached = product((q_ref[:, columns(head)],), split(state_ref[head]), NN)
        out = out_ref[head] + jnp.exp(spread_ref[head]) * scale * reached
        out_ref[head] = out
        gained = grad_ref[:, columns(head)].astype(F32) * gain_ref[row(head), :]
        norm_ref[side, 0] += out * out
        norm_ref[side, 1] += gained * out

    for chunk in range(share):
        forward.arrive(chunk)
        each_head(chunk, whole_out)

    norm_copies = to_peers(norm_ref, side, side_peers, "head", norm_sems)
    for copy in norm_copies:
        copy.start()
    for copy in norm_copies:
        copy.wait_recv()
    squares, inners = norm_ref[0, 0], norm_ref[0, 1]
    for place in range(1, split_heads):
        squares, inners = squares + norm_ref[place, 0], inners + norm_ref[place, 1]
    rms = jnp.sqrt(jnp.sum(squares, axis=1, keepdims=True) / full_width + EPS)
    bent = jnp.sum(inners, axis=1, keepdims=True) / (full_width * rms * rms * rms)
    scale_ref[0] = jnp.broadcast_to(1.0 / rms, (length, DK))
    scale_ref[1] = jnp.broadcast_to(bent, (length, DK))

    def own_start(head):
        grads = grad_ref[:, columns(head)].astype(F32)
        gain = gain_ref[row(head), :]
        out = out_ref[head]
        normed = out * scale_ref[0]
        adjoint = grads * gain * scale_ref[0] - out * scale_ref[1]
        adjoint_ref[head] = adjoint
        weighted = adjoint * jnp.exp(spread_ref[head]) * scale
        start_ref[head] = product((q_ref[:, columns(head)],), split(weighted), TN)
        y_ref[:, columns(head)] = (normed * gain).astype(BF16)
        gain_ref_in[inner, row(head), :] = jnp.sum(grads * normed, axis=0, keepdims=True)

    for chunk in range(share):
        each_head(chunk, own_start)
        backward.deal(chunk)
    gain_copies_in = to_peers(gain_ref_in, inner, inner_peers, "tm", gain_sems_in)
    for copy in gain_copies_in:
        copy.start()

    def own_grads(head):
        queries, keys = q_ref[:, columns(head)], k_ref[:, columns(head)]
        adjoint = split(adjoint_ref[head])
        pairs = split(product(adjoint, (v_ref[:, columns(head)],), NT) * weight_ref[head])
        reached = product(adjoint, split(state_ref[head]), NT) * jnp.exp(spread_ref[head])
        q_grad = (product(pairs, (keys,), NN) + reached) * scale
        q_grad_ref[:, columns(head)] = q_grad.astype(BF16)
        k_part_ref[head] = product(pairs, (queries,), TN) * scale
        v_part_ref[head] = product(split(score_ref[head]), adjoint, TN)

    for chunk in range(share):
        each_head(chunk, own_grads)
        backward.combine(chunk)

    for copy in gain_copies_in:
        copy.wait_recv()
    gain_sum = gain_ref_in[0]
    for place in range(1, group):
        gain_sum = gain_sum + gain_ref_in[place]
    gain_ref_out[outer] = gain_sum
    gain_copies_out = to_peers(gain_ref_out, outer, outer_peers, "tm", gain_sems_out)
    for copy in gain_copies_out:
        copy.start()

    ones = jnp.ones((16, DK), BF16)
    ends_here = rows_at == length - 1

    def whole_grads(head):
        later = later_ref[head]
        parts = split(later)
        keys = k_ref[:, columns(head)]
        tail = jnp.exp(total_ref[row(head), :] - spread_ref[head])
        k_grad = k_part_ref[head] + tail * product((v_ref[:, columns(head)],), parts, NT)
        v_grad = v_part_ref[head] + tail * product((keys,), parts, NN)
        k_grad_ref[:, columns(head)] = k_grad.astype(BF16)
        v_grad_ref[:, columns(head)] = v_grad.astype(BF16)
        after = state_ref[head] * jnp.exp(total_ref[row(head), :]) + end_ref[head]
        at_end = jnp.sum(after * later, axis=0, keepdims=True)
        change = out_ref[head] * adjoint_ref[head] - keys.astype(F32) * k_grad
        change = change + jnp.where(ends_here, at_end, 0.0)
        change_ref[row(head), :] = product((ones,), split(change, 3), NT)[:1]

    for chunk in range(share):
        backward.arrive(chunk)
        each_head(chunk, whole_grads)
    from_here = jnp.where(rows_at >= lanes_at, 1.0, 0.0).astype(BF16)
    decay_grad_ref[...] = product(split(change_ref[...], 3), (from_here,), NN)

    for copy in gain_copies_out:
        copy.wait_recv()
    gain_sum = gain_ref_out[0]
    for place in range(1, chain):
        gain_sum = gain_sum + gain_ref_out[place]
    gain_grad_ref[...] = gain_sum

    forward.finish()
    backward.finish()
    for copy in factor_copies + norm_copies + gain_copies_in + gain_copies_out:
        copy.wait_send()


def body(group, chain, split_heads, queries, keys, values, log_decay, agent_ids, norm_gain, out_grad):
    length, width = queries.shape
    heads = width // DK
    share = heads // group
    state = (DK, DK)
    row_shape = (heads, DK)
    travelling = [
        pltpu.VMEM((heads, *state), F32),
        pltpu.VMEM((group, share, *state), F32),
        pltpu.VMEM((share, *state), F32),
        pltpu.VMEM((share, *state), F32),
        pltpu.VMEM((group, share, *state), F32),
        pltpu.VMEM((heads, *state), F32),
    ]
    per_head = pltpu.VMEM((heads, length, DK), F32)
    peers, others, sides = max(1, group - 1), max(1, chain - 1), max(1, split_heads - 1)
    wide = jax.ShapeDtypeStruct((length, width), BF16)
    outs = pl.pallas_call(
        functools.partial(kernel, group, chain, split_heads),
        out_shape=[
            wide,
            wide,
            wide,
            wide,
            jax.ShapeDtypeStruct((heads, length), F32),
            jax.ShapeDtypeStruct((heads, DK), F32),
        ],
        in_specs=[pl.BlockSpec(memory_space=pltpu.VMEM)] * 7,
        out_specs=[pl.BlockSpec(memory_space=pltpu.VMEM)] * 6,
        scratch_shapes=[
            pltpu.VMEM(row_shape, F32),
            pltpu.VMEM(row_shape, F32),
            per_head,
            pltpu.VMEM((length, length), F32),
            pltpu.VMEM((group, *row_shape), F32),
            per_head,
            per_head,
            per_head,
            per_head,
            per_head,
            per_head,
            pltpu.VMEM((split_heads, 2, length, DK), F32),
            pltpu.VMEM((2, length, DK), F32),
            pltpu.VMEM(row_shape, F32),
            pltpu.VMEM((group, *row_shape), F32),
            pltpu.VMEM((chain, *row_shape), F32),
            *travelling,
            *travelling,
            pltpu.SemaphoreType.DMA((2, 2, 2, peers, share)),
            pltpu.SemaphoreType.DMA((2, 2, share)),
            pltpu.SemaphoreType.DMA((2, peers)),
            pltpu.SemaphoreType.DMA((2, sides)),
            pltpu.SemaphoreType.DMA((2, peers)),
            pltpu.SemaphoreType.DMA((2, others)),
        ],
        compiler_params=pltpu.CompilerParams(
            collective_id=0, has_side_effects=True, vmem_limit_bytes=48 * 2**20
        ),
        cost_estimate=pl.CostEstimate(
            flops=heads * 28 * 2 * DK**3,
            bytes_accessed=8 * length * width * 2,
            transcendentals=heads * 5 * DK**2,
        ),
    )(
        queries,
        keys,
        values,
        log_decay,
        agent_ids.reshape(1, length),
        norm_gain.reshape(heads, DK),
        out_grad,
    )
    return (*outs[:5], outs[5].reshape(width))


def solution(mesh):
    count, split_heads = mesh.shape["tm"], mesh.shape["head"]

    def placed_body(queries, *rest):
        group = math.gcd(math.gcd(count, queries.shape[1] // DK), 4)
        return body(group, count // group, split_heads, queries, *rest)

    wide = P("tm", "head")
    return jax.shard_map(
        placed_body,
        mesh=mesh,
        in_specs=(wide, wide, wide, P("head", "tm"), P("tm"), P("head"), wide),
        out_specs=(wide, wide, wide, wide, P("head", "tm"), P("head")),
        check_vma=False,
    )
```

time: 394 us -> 78.1 us (0.20)
  waiting for transfers between devices: 233 us -> 0 us
  Pallas kernels: 0 us -> 66.5 us
  blocking collectives: 56.9 us -> 0 us
  starting transfers between devices: 46.9 us -> 0 us
  matrix products: 29.9 us -> 0 us
  other arithmetic: 14.1 us -> 0 us
    ppermute x16 -> x0, waiting for transfers between devices: 233 us -> none  [passed_along(): lax.ppermute(value, axis, [(source, source + steps) for source in range(l...]
    pallas_call x0 -> x1, Pallas kernels: none -> 66.5 us  [body(): pl.pallas_call(functools.partial(kernel, group, chain, split_heads), out_...]
    psum x3 -> x0, blocking collectives: 56.9 us -> none  [the longest x1 52 us: body(): gain_grad = lax.psum(jnp.sum(grad_rows * normed, axis=0), 'tm')]
    ppermute x16 -> x0, starting transfers between devices: 46.9 us -> none  [passed_along(): lax.ppermute(value, axis, [(source, source + steps) for source in range(l...]
    dot_general x14 -> x0, matrix products: 29.9 us -> none  [the longest x3 8.48 us: advance(): output = jnp.einsum('hts,she->the', scores, value_block, precision=HIGH)]
    unnamed x34 -> x20, local copies, waits for them, and re-layouts: 5.95 us -> 10.6 us
    add x9 -> x0, other arithmetic: 3.98 us -> none  [the longest x8 3.3 us: combine(): later[0][:, None, None] * earlier[1] + later[1]]
  transfers between devices with their start and end apart: 16 -> 0, of which waited for: 12 -> 0; matrix products, arithmetic and copies ran while one was open for 6% -> 0% of each run, Pallas kernels for 0% -> 0%
where the time goes in v1:
time: 78.1 us; the launch traced here: 77.7 us
  Pallas kernels  66.5 us (85%)
  local copies, waits for them, and re-layouts  10.6 us (14%)
    pallas_call x1, Pallas kernels, body(): pl.pallas_call(functools.partial(kernel, group, chain, split_heads), out_...  66.5 us
    unnamed x20, local copies, waits for them, and re-layouts  10.6 us

profile of v1, /device:TPU:0, one launch (start us, length us, event | category | flops | bytes accessed | tf_op | source)
XLA Modules:
  0.0 77.7 jit_solution(6119187227834392090)
XLA Ops:
  0.6 0.0 copy-start.6
  0.6 0.6 copy-done.6
  1.3 0.0 copy-start
  1.3 1.0 %copy-done = bf16[128,2048]{1,0:T(8,128)(2,1)S(1)} copy-done((bf16[128,2048]{1,0:T(8,128)(2,1)S(1)}, bf16[128,2048]{1,0:T(8,128)(2,1)}, u32[]{:S(2)}) %copy-start) | copy-done | bytes 524312
  2.3 0.0 copy-start.1
  2.3 1.0 %copy-done.1 = bf16[128,2048]{1,0:T(8,128)(2,1)S(1)} copy-done((bf16[128,2048]{1,0:T(8,128)(2,1)S(1)}, bf16[128,2048]{1,0:T(8,128)(2,1)}, u32[]{:S(2)}) %copy-start.1) | copy-done | bytes 524312
  3.4 0.0 copy-start.2
  3.4 1.0 %copy-done.2 = bf16[128,2048]{1,0:T(8,128)(2,1)S(1)} copy-done((bf16[128,2048]{1,0:T(8,128)(2,1)S(1)}, bf16[128,2048]{1,0:T(8,128)(2,1)}, u32[]{:S(2)}) %copy-start.2) | copy-done | bytes 524312
  4.4 0.0 copy-start.3
  4.4 1.0 %copy-done.3 = bf16[128,2048]{1,0:T(8,128)(2,1)S(1)} copy-done((bf16[128,2048]{1,0:T(8,128)(2,1)S(1)}, bf16[128,2048]{1,0:T(8,128)(2,1)}, u32[]{:S(2)}) %copy-start.3) | copy-done | bytes 524312
  5.5 0.0 copy-start.4
  5.5 0.7 copy-done.4
  6.2 0.0 copy-start.5
  6.2 0.7 copy-done.5
  6.9 66.5 %shard_map.118 = (bf16[128,2048]{1,0:T(8,128)(2,1)S(1)}, bf16[128,2048]{1,0:T(8,128)(2,1)S(1)}, bf16[128,2048]{1,0:T(8,128)(2,1)S(1)}, bf16[128,2048]{1,0:T(8,12...) custom-call(bf16[128,2048]{1,0:T(8,128)(2,1)S(1)} %copy-done, bf16[128,2048]{1,0:T(8,128)(2,1)S(1)} %copy-done.1, ...), custom_call_target="tpu_custom_call" | custom-call | flops 1879048192 | bytes 4194304 | tf_op jit(solution)/shard_map/pallas_call | solution.py:395
  73.4 0.8 %copy.19 = bf16[128,2048]{1,0:T(8,128)(2,1)} copy(bf16[128,2048]{1,0:T(8,128)(2,1)S(1)} %get-tuple-element.24) | data formatting | bytes 1048576
  74.2 0.8 %copy.20 = bf16[128,2048]{1,0:T(8,128)(2,1)} copy(bf16[128,2048]{1,0:T(8,128)(2,1)S(1)} %get-tuple-element.25) | data formatting | bytes 1048576
  74.9 0.8 %copy.21 = bf16[128,2048]{1,0:T(8,128)(2,1)} copy(bf16[128,2048]{1,0:T(8,128)(2,1)S(1)} %get-tuple-element.26) | data formatting | bytes 1048576
  75.7 0.8 %copy.22 = bf16[128,2048]{1,0:T(8,128)(2,1)} copy(bf16[128,2048]{1,0:T(8,128)(2,1)S(1)} %get-tuple-element.27) | data formatting | bytes 1048576
  76.5 0.6 copy.23
  77.1 0.6 copy.24
Async XLA Ops:
  0.6 0.7 copy-start.6
  1.3 1.0 %copy-start = (bf16[128,2048]{1,0:T(8,128)(2,1)S(1)}, bf16[128,2048]{1,0:T(8,128)(2,1)}, u32[]{:S(2)}) copy-start(bf16[128,2048]{1,0:T(8,128)(2,1)} %q_ref.1) | copy-start | bytes 1572868
  2.3 1.0 %copy-start.1 = (bf16[128,2048]{1,0:T(8,128)(2,1)S(1)}, bf16[128,2048]{1,0:T(8,128)(2,1)}, u32[]{:S(2)}) copy-start(bf16[128,2048]{1,0:T(8,128)(2,1)} %k_ref.1) | copy-start | bytes 1572868
  3.4 1.0 %copy-start.2 = (bf16[128,2048]{1,0:T(8,128)(2,1)S(1)}, bf16[128,2048]{1,0:T(8,128)(2,1)}, u32[]{:S(2)}) copy-start(bf16[128,2048]{1,0:T(8,128)(2,1)} %v_ref.1) | copy-start | bytes 1572868
  4.4 1.0 %copy-start.3 = (bf16[128,2048]{1,0:T(8,128)(2,1)S(1)}, bf16[128,2048]{1,0:T(8,128)(2,1)}, u32[]{:S(2)}) copy-start(bf16[128,2048]{1,0:T(8,128)(2,1)} %grad_ref.1) | copy-start | bytes 1572868
  5.5 0.7 copy-start.4
  6.2 0.7 copy-start.5

commit v2 on v1

--- a/solution.py
+++ b/solution.py
@@ -11,7 +11,7 @@
 DK = 128
 TEAM = 16
 EPS = 1e-06
-UNROLL = 2
+UNROLL = 4
 MESH = pl.DeviceIdType.MESH
 F32, BF16 = jnp.float32, jnp.bfloat16
 NN, NT, TN = ((1,), (0,)), ((1,), (1,)), ((0,), (0,))
@@ -162,14 +162,31 @@
 
 def kernel(
     group, chain, split_heads,
+    q_from, k_from, v_from, decay_from, agent_from, gain_from, grad_from,
+    y_ref, q_grad_ref, k_grad_ref, v_grad_ref, decay_grad_ref, gain_grad_ref,
     q_ref, k_ref, v_ref, decay_ref, agent_ref, gain_ref, grad_ref,
-    y_ref, q_grad_ref, k_grad_ref, v_grad_ref, decay_grad_ref, gain_grad_ref,
     sum_ref, total_ref, spread_ref, bias_ref, factor_ref, score_ref, weight_ref, out_ref, adjoint_ref,
     k_part_ref, v_part_ref, norm_ref, scale_ref, change_ref, gain_ref_in, gain_ref_out,
     end_ref, dealt_ref, came_ref, gone_ref, given_ref, state_ref,
     start_ref, dealt_back_ref, came_back_ref, gone_back_ref, given_back_ref, later_ref,
-    scan_sems, chain_sems, factor_sems, norm_sems, gain_sems_in, gain_sems_out,
+    load_sems, scan_sems, chain_sems, factor_sems, norm_sems, gain_sems_in, gain_sems_out,
 ):
+    loads = [
+        pltpu.make_async_copy(source, target, load_sems.at[number])
+        for number, (source, target) in enumerate(
+            [
+                (decay_from, decay_ref),
+                (k_from, k_ref),
+                (v_from, v_ref),
+                (q_from, q_ref),
+                (agent_from, agent_ref),
+                (gain_from, gain_ref),
+                (grad_from, grad_ref),
+            ]
+        )
+    ]
+    for load in loads:
+        load.start()
     length, width = q_ref.shape
     heads = width // DK
     share = heads // group
@@ -227,14 +244,12 @@
 
     rows_at = lax.broadcasted_iota(jnp.int32, (length, length), 0)
     lanes_at = lax.broadcasted_iota(jnp.int32, (length, length), 1)
+    loads[0].wait()
     decays = split(decay_ref[...], 3)
     up_to = jnp.where(rows_at <= lanes_at, 1.0, 0.0).astype(BF16)
     sum_ref[...] = product(decays, (up_to,), NN)
     total_ref[...] = product(decays, (jnp.ones((length, DK), BF16),), NN)
     factor_ref[inner] = jnp.exp(total_ref[...])
-    teams = jnp.broadcast_to(lax.div(agent_ref[...], TEAM).astype(F32), (length, length))
-    visible = (rows_at >= lanes_at) & (teams == teams.T)
-    bias_ref[...] = jnp.where(visible, 0.0, -1e30)
 
     def own_end(head):
         across = jnp.broadcast_to(sum_ref[row(head), :], (length, length))
@@ -244,6 +259,8 @@
         keys = k_ref[:, columns(head)].astype(F32) * tail
         end_ref[head] = product(split(keys), (v_ref[:, columns(head)],), TN)
 
+    for load in loads[1:3]:
+        load.wait()
     each_head(0, own_end)
     pl.semaphore_wait(barrier, len(inner_peers) + len(outer_peers) + len(side_peers))
     factor_copies = to_peers(factor_ref, inner, inner_peers, "tm", factor_sems)
@@ -254,6 +271,12 @@
         each_head(chunk, own_end)
         forward.deal(chunk)
 
+    for load in loads[3:]:
+        load.wait()
+    teams = jnp.broadcast_to(lax.div(agent_ref[...], TEAM).astype(F32), (length, length))
+    visible = (rows_at >= lanes_at) & (teams == teams.T)
+    bias_ref[...] = jnp.where(visible, 0.0, -1e30)
+
     def own_out(head):
         across = sum_ref[row(head), :]
         weight = jnp.exp(spread_ref[head] - across + bias_ref[...])
@@ -265,8 +288,8 @@
     for copy in factor_copies:
         copy.wait_recv()
     for chunk in range(share):
+        forward.combine(chunk)
         each_head(chunk, own_out)
-        forward.combine(chunk)
 
     norm_ref[side] = jnp.zeros_like(norm_ref[side])
 
@@ -296,20 +319,24 @@
     scale_ref[1] = jnp.broadcast_to(bent, (length, DK))
 
     def own_start(head):
-        grads = grad_ref[:, columns(head)].astype(F32)
-        gain = gain_ref[row(head), :]
-        out = out_ref[head]
-        normed = out * scale_ref[0]
-        adjoint = grads * gain * scale_ref[0] - out * scale_ref[1]
+        gained = grad_ref[:, columns(head)].astype(F32) * gain_ref[row(head), :]
+        adjoint = gained * scale_ref[0] - out_ref[head] * scale_ref[1]
         adjoint_ref[head] = adjoint
         weighted = adjoint * jnp.exp(spread_ref[head]) * scale
         start_ref[head] = product((q_ref[:, columns(head)],), split(weighted), TN)
-        y_ref[:, columns(head)] = (normed * gain).astype(BF16)
-        gain_ref_in[inner, row(head), :] = jnp.sum(grads * normed, axis=0, keepdims=True)
 
     for chunk in range(share):
         each_head(chunk, own_start)
         backward.deal(chunk)
+
+    def result(head):
+        normed = out_ref[head] * scale_ref[0]
+        y_ref[:, columns(head)] = (normed * gain_ref[row(head), :]).astype(BF16)
+        grads = grad_ref[:, columns(head)].astype(F32)
+        gain_ref_in[inner, row(head), :] = jnp.sum(grads * normed, axis=0, keepdims=True)
+
+    for chunk in range(share):
+        each_head(chunk, result)
     gain_copies_in = to_peers(gain_ref_in, inner, inner_peers, "tm", gain_sems_in)
     for copy in gain_copies_in:
         copy.start()
@@ -325,8 +352,8 @@
         v_part_ref[head] = product(split(score_ref[head]), adjoint, TN)
 
     for chunk in range(share):
+        backward.combine(chunk)
         each_head(chunk, own_grads)
-        backward.combine(chunk)
 
     for copy in gain_copies_in:
         copy.wait_recv()
@@ -373,6 +400,19 @@
     backward.finish()
     for copy in factor_copies + norm_copies + gain_copies_in + gain_copies_out:
         copy.wait_send()
+
+
+def writer(*refs):
+    *arrays, sems = refs
+    half = len(arrays) // 2
+    copies = [
+        pltpu.make_async_copy(source, target, sems.at[number])
+        for number, (source, target) in enumerate(zip(arrays[:half], arrays[half:]))
+    ]
+    for copy in copies:
+        copy.start()
+    for copy in copies:
+        copy.wait()
 
 
 def body(group, chain, split_heads, queries, keys, values, log_decay, agent_ids, norm_gain, out_grad):
@@ -402,9 +442,14 @@
             jax.ShapeDtypeStruct((heads, length), F32),
             jax.ShapeDtypeStruct((heads, DK), F32),
         ],
-        in_specs=[pl.BlockSpec(memory_space=pltpu.VMEM)] * 7,
+        in_specs=[pl.BlockSpec(memory_space=pltpu.HBM)] * 7,
         out_specs=[pl.BlockSpec(memory_space=pltpu.VMEM)] * 6,
         scratch_shapes=[
+            *[pltpu.VMEM((length, width), BF16)] * 3,
+            pltpu.VMEM((heads, length), F32),
+            pltpu.VMEM((1, length), agent_ids.dtype),
+            pltpu.VMEM(row_shape, F32),
+            pltpu.VMEM((length, width), BF16),
             pltpu.VMEM(row_shape, F32),
             pltpu.VMEM(row_shape, F32),
             per_head,
@@ -423,6 +468,7 @@
             pltpu.VMEM((chain, *row_shape), F32),
             *travelling,
             *travelling,
+            pltpu.SemaphoreType.DMA((7,)),
             pltpu.SemaphoreType.DMA((2, 2, 2, peers, share)),
             pltpu.SemaphoreType.DMA((2, 2, share)),
             pltpu.SemaphoreType.DMA((2, peers)),
@@ -447,6 +493,13 @@
         norm_gain.reshape(heads, DK),
         out_grad,
     )
+    outs = pl.pallas_call(
+        writer,
+        out_shape=[jax.ShapeDtypeStruct(out.shape, out.dtype) for out in outs],
+        in_specs=[pl.BlockSpec(memory_space=pltpu.VMEM)] * 6,
+        out_specs=[pl.BlockSpec(memory_space=pltpu.HBM)] * 6,
+        scratch_shapes=[pltpu.SemaphoreType.DMA((6,))],
+    )(*outs)
     return (*outs[:5], outs[5].reshape(width))
 
 

time: 78.1 us -> 80.7 us (1.033)
  Pallas kernels: 66.5 us -> 69 us
    pallas_call x0 -> x1, Pallas kernels: none -> 2.88 us  [body(): pl.pallas_call(writer, out_shape=[jax.ShapeDtypeStruct(out.shape, out.dty...]
    unnamed x20 -> x26, local copies, waits for them, and re-layouts: 10.6 us -> 10.6 us
where the time goes in v2:
time: 80.7 us; the launch traced here: 80.3 us
  Pallas kernels  69 us (86%)
  local copies, waits for them, and re-layouts  10.6 us (13%)
    pallas_call x1, Pallas kernels, body(): pl.pallas_call(functools.partial(kernel, group, chain, split_heads), out_...  66.1 us
    unnamed x26, local copies, waits for them, and re-layouts  10.6 us
    pallas_call x1, Pallas kernels, body(): pl.pallas_call(writer, out_shape=[jax.ShapeDtypeStruct(out.shape, out.dty...  2.88 us

profile of v2, /device:TPU:0, one launch (start us, length us, event | category | flops | bytes accessed | tf_op | source)
XLA Modules:
  0.0 80.3 jit_solution(18399157655884193657)
XLA Ops:
  0.6 0.0 copy-start.12
  0.6 0.6 copy-done.12
  1.3 0.0 copy-start.6
  1.3 1.0 %copy-done.6 = bf16[128,2048]{1,0:T(8,128)(2,1)S(1)} copy-done((bf16[128,2048]{1,0:T(8,128)(2,1)S(1)}, bf16[128,2048]{1,0:T(8,128)(2,1)}, u32[]{:S(2)}) %copy-start.6) | copy-done | bytes 524312
  2.3 0.0 copy-start.7
  2.3 1.0 %copy-done.7 = bf16[128,2048]{1,0:T(8,128)(2,1)S(1)} copy-done((bf16[128,2048]{1,0:T(8,128)(2,1)S(1)}, bf16[128,2048]{1,0:T(8,128)(2,1)}, u32[]{:S(2)}) %copy-start.7) | copy-done | bytes 524312
  3.4 0.0 copy-start.8
  3.4 1.0 %copy-done.8 = bf16[128,2048]{1,0:T(8,128)(2,1)S(1)} copy-done((bf16[128,2048]{1,0:T(8,128)(2,1)S(1)}, bf16[128,2048]{1,0:T(8,128)(2,1)}, u32[]{:S(2)}) %copy-start.8) | copy-done | bytes 524312
  4.4 0.0 copy-start.9
  4.4 1.0 %copy-done.9 = bf16[128,2048]{1,0:T(8,128)(2,1)S(1)} copy-done((bf16[128,2048]{1,0:T(8,128)(2,1)S(1)}, bf16[128,2048]{1,0:T(8,128)(2,1)}, u32[]{:S(2)}) %copy-start.9) | copy-done | bytes 524312
  5.5 0.0 copy-start.10
  5.5 0.7 copy-done.10
  6.2 0.0 copy-start.11
  6.2 0.7 copy-done.11
  6.9 66.1 %shard_map.118 = (bf16[128,2048]{1,0:T(8,128)(2,1)S(1)}, bf16[128,2048]{1,0:T(8,128)(2,1)S(1)}, bf16[128,2048]{1,0:T(8,128)(2,1)S(1)}, bf16[128,2048]{1,0:T(8,12...) custom-call(bf16[128,2048]{1,0:T(8,128)(2,1)S(1)} %copy-done.6, bf16[128,2048]{1,0:T(8,128)(2,1)S(1)} %copy-done.7, ...), custom_call_target="tpu_custom_call" | custom-call | flops 1879048192 | bytes 4194304 | tf_op jit(solution)/shard_map/pallas_call | solution.py:435
  73.0 0.0 copy-start
  73.0 0.8 copy-done
  73.8 0.0 copy-start.1
  73.8 0.8 copy-done.1
  74.6 0.0 copy-start.2
  74.6 0.8 %copy-done.2 = bf16[128,2048]{1,0:T(8,128)(2,1)} copy-done((bf16[128,2048]{1,0:T(8,128)(2,1)}, bf16[128,2048]{1,0:T(8,128)(2,1)S(1)}, u32[]{:S(2)}) %copy-start.2) | copy-done | bytes 524312
  75.4 0.0 copy-start.3
  75.4 0.8 copy-done.3
  76.2 0.0 copy-start.4
  76.2 0.6 copy-done.4
  76.8 0.0 copy-start.5
  76.8 0.6 copy-done.5
  77.4 2.9 %shard_map.119 = (bf16[128,2048]{1,0:T(8,128)(2,1)}, bf16[128,2048]{1,0:T(8,128)(2,1)}, bf16[128,2048]{1,0:T(8,128)(2,1)}, bf16[128,2048]{1,0:T(8,128)(2,1)}, f32[16,128]{1,0:T(8,128)}, /*index=5*/f32[16,128]{1,0:T(8,128)}) custom-call(bf16[128,2048]{1,0:T(8,128)(2,1)} %copy-done, bf16[128,2048]{1,0:T(8,128)(2,1)} %copy-done.1, bf16[128,2048]{1,0:T(8,128)(2,1)} %copy-done.2, ...), custom_call_target="tpu_custom_call" | custom-call | tf_op jit(solution)/shard_map/pallas_call | solution.py:496
Async XLA Ops:
  0.6 0.7 copy-start.12
  1.3 1.0 %copy-start.6 = (bf16[128,2048]{1,0:T(8,128)(2,1)S(1)}, bf16[128,2048]{1,0:T(8,128)(2,1)}, u32[]{:S(2)}) copy-start(bf16[128,2048]{1,0:T(8,128)(2,1)} %q_from.1) | copy-start | bytes 1572868
  2.3 1.0 %copy-start.7 = (bf16[128,2048]{1,0:T(8,128)(2,1)S(1)}, bf16[128,2048]{1,0:T(8,128)(2,1)}, u32[]{:S(2)}) copy-start(bf16[128,2048]{1,0:T(8,128)(2,1)} %k_from.1) | copy-start | bytes 1572868
  3.4 1.0 %copy-start.8 = (bf16[128,2048]{1,0:T(8,128)(2,1)S(1)}, bf16[128,2048]{1,0:T(8,128)(2,1)}, u32[]{:S(2)}) copy-start(bf16[128,2048]{1,0:T(8,128)(2,1)} %v_from.1) | copy-start | bytes 1572868
  4.4 1.0 %copy-start.9 = (bf16[128,2048]{1,0:T(8,128)(2,1)S(1)}, bf16[128,2048]{1,0:T(8,128)(2,1)}, u32[]{:S(2)}) copy-start(bf16[128,2048]{1,0:T(8,128)(2,1)} %grad_from.1) | copy-start | bytes 1572868
  5.5 0.7 copy-start.10
  6.2 0.7 copy-start.11
  73.0 0.8 copy-start
  73.8 0.8 copy-start.1
  74.6 0.8 %copy-start.2 = (bf16[128,2048]{1,0:T(8,128)(2,1)}, bf16[128,2048]{1,0:T(8,128)(2,1)S(1)}, u32[]{:S(2)}) copy-start(bf16[128,2048]{1,0:T(8,128)(2,1)S(1)} %get-tuple-element.20.refs_2_) | copy-start | bytes 1572868
  75.4 0.8 copy-start.3
  76.2 0.6 copy-start.4
  76.8 0.6 copy-start.5

commit v3 on v2

--- a/solution.py
+++ b/solution.py
@@ -163,13 +163,14 @@
 def kernel(
     group, chain, split_heads,
     q_from, k_from, v_from, decay_from, agent_from, gain_from, grad_from,
+    y_to, q_grad_to, k_grad_to, v_grad_to, decay_grad_to, gain_grad_to,
+    q_ref, k_ref, v_ref, decay_ref, agent_ref, gain_ref, grad_ref,
     y_ref, q_grad_ref, k_grad_ref, v_grad_ref, decay_grad_ref, gain_grad_ref,
-    q_ref, k_ref, v_ref, decay_ref, agent_ref, gain_ref, grad_ref,
     sum_ref, total_ref, spread_ref, bias_ref, factor_ref, score_ref, weight_ref, out_ref, adjoint_ref,
     k_part_ref, v_part_ref, norm_ref, scale_ref, change_ref, gain_ref_in, gain_ref_out,
     end_ref, dealt_ref, came_ref, gone_ref, given_ref, state_ref,
     start_ref, dealt_back_ref, came_back_ref, gone_back_ref, given_back_ref, later_ref,
-    load_sems, scan_sems, chain_sems, factor_sems, norm_sems, gain_sems_in, gain_sems_out,
+    load_sems, store_sems, scan_sems, chain_sems, factor_sems, norm_sems, gain_sems_in, gain_sems_out,
 ):
     loads = [
         pltpu.make_async_copy(source, target, load_sems.at[number])
@@ -187,6 +188,19 @@
     ]
     for load in loads:
         load.start()
+    stores = [
+        pltpu.make_async_copy(source, target, store_sems.at[number])
+        for number, (source, target) in enumerate(
+            [
+                (y_ref, y_to),
+                (q_grad_ref, q_grad_to),
+                (k_grad_ref, k_grad_to),
+                (v_grad_ref, v_grad_to),
+                (decay_grad_ref, decay_grad_to),
+                (gain_grad_ref, gain_grad_to),
+            ]
+        )
+    ]
     length, width = q_ref.shape
     heads = width // DK
     share = heads // group
@@ -337,6 +351,7 @@
 
     for chunk in range(share):
         each_head(chunk, result)
+    stores[0].start()
     gain_copies_in = to_peers(gain_ref_in, inner, inner_peers, "tm", gain_sems_in)
     for copy in gain_copies_in:
         copy.start()
@@ -354,6 +369,7 @@
     for chunk in range(share):
         backward.combine(chunk)
         each_head(chunk, own_grads)
+    stores[1].start()
 
     for copy in gain_copies_in:
         copy.wait_recv()
@@ -386,8 +402,11 @@
     for chunk in range(share):
         backward.arrive(chunk)
         each_head(chunk, whole_grads)
+    stores[2].start()
+    stores[3].start()
     from_here = jnp.where(rows_at >= lanes_at, 1.0, 0.0).astype(BF16)
     decay_grad_ref[...] = product(split(change_ref[...], 3), (from_here,), NN)
+    stores[4].start()
 
     for copy in gain_copies_out:
         copy.wait_recv()
@@ -395,11 +414,14 @@
     for place in range(1, chain):
         gain_sum = gain_sum + gain_ref_out[place]
     gain_grad_ref[...] = gain_sum
+    stores[5].start()
 
     forward.finish()
     backward.finish()
     for copy in factor_copies + norm_copies + gain_copies_in + gain_copies_out:
         copy.wait_send()
+    for store in stores:
+        store.wait()
 
 
 def writer(*refs):
@@ -443,13 +465,16 @@
             jax.ShapeDtypeStruct((heads, DK), F32),
         ],
         in_specs=[pl.BlockSpec(memory_space=pltpu.HBM)] * 7,
-        out_specs=[pl.BlockSpec(memory_space=pltpu.VMEM)] * 6,
+        out_specs=[pl.BlockSpec(memory_space=pltpu.HBM)] * 6,
         scratch_shapes=[
             *[pltpu.VMEM((length, width), BF16)] * 3,
             pltpu.VMEM((heads, length), F32),
             pltpu.VMEM((1, length), agent_ids.dtype),
             pltpu.VMEM(row_shape, F32),
             pltpu.VMEM((length, width), BF16),
+            *[pltpu.VMEM((length, width), BF16)] * 4,
+            pltpu.VMEM((heads, length), F32),
+            pltpu.VMEM(row_shape, F32),
             pltpu.VMEM(row_shape, F32),
             pltpu.VMEM(row_shape, F32),
             per_head,
@@ -469,6 +494,7 @@
             *travelling,
             *travelling,
             pltpu.SemaphoreType.DMA((7,)),
+            pltpu.SemaphoreType.DMA((6,)),
             pltpu.SemaphoreType.DMA((2, 2, 2, peers, share)),
             pltpu.SemaphoreType.DMA((2, 2, share)),
             pltpu.SemaphoreType.DMA((2, peers)),
@@ -477,7 +503,7 @@
             pltpu.SemaphoreType.DMA((2, others)),
         ],
         compiler_params=pltpu.CompilerParams(
-            collective_id=0, has_side_effects=True, vmem_limit_bytes=48 * 2**20
+            collective_id=0, has_side_effects=True, vmem_limit_bytes=60 * 2**20
         ),
         cost_estimate=pl.CostEstimate(
             flops=heads * 28 * 2 * DK**3,
@@ -496,9 +522,10 @@
     outs = pl.pallas_call(
         writer,
         out_shape=[jax.ShapeDtypeStruct(out.shape, out.dtype) for out in outs],
-        in_specs=[pl.BlockSpec(memory_space=pltpu.VMEM)] * 6,
+        in_specs=[pl.BlockSpec(memory_space=pltpu.HBM)] * 6,
         out_specs=[pl.BlockSpec(memory_space=pltpu.HBM)] * 6,
         scratch_shapes=[pltpu.SemaphoreType.DMA((6,))],
+        compiler_params=pltpu.CompilerParams(vmem_limit_bytes=60 * 2**20),
     )(*outs)
     return (*outs[:5], outs[5].reshape(width))
 

time: 80.7 us -> 133 us (1.65)
  Pallas kernels: 69 us -> 132 us
  local copies, waits for them, and re-layouts: 10.6 us -> 0 us
    pallas_call x1, Pallas kernels: 2.88 us -> 65.2 us  [body(): pl.pallas_call(writer, out_shape=[jax.ShapeDtypeStruct(out.shape, out.dty...]
    unnamed x26 -> x0, local copies, waits for them, and re-layouts: 10.6 us -> none
where the time goes in v3:
time: 133 us; the launch traced here: 132 us
  Pallas kernels  132 us (99%)
    pallas_call x1, Pallas kernels, body(): pl.pallas_call(functools.partial(kernel, group, chain, split_heads), out_...  66.7 us
    pallas_call x1, Pallas kernels, body(): pl.pallas_call(writer, out_shape=[jax.ShapeDtypeStruct(out.shape, out.dty...  65.2 us

profile of v3, /device:TPU:0, one launch (start us, length us, event | category | flops | bytes accessed | tf_op | source)
XLA Modules:
  0.0 132.5 jit_solution(8823145448704130752)
XLA Ops:
  0.6 66.7 %shard_map.118 = (bf16[128,2048]{1,0:T(8,128)(2,1)}, bf16[128,2048]{1,0:T(8,128)(2,1)}, bf16[128,2048]{1,0:T(8,128)(2,1)}, bf16[128,2048]{1,0:T(8,128)(2,1)}, f32[16,128]{1,0:T(8,128)}, /*index=5*/f32[16,128]{1,0:T(8,128)}) custom-call(bf16[128,2048]{1,0:T(8,128)(2,1)} %q_from.1, bf16[128,2048]{1,0:T(8,128)(2,1)} %k_from.1, bf16[128,2048]{1,0:T(8,128)(2,1)} %v_from.1, ...), custom_call_target="tpu_custom_call" | custom-call | flops 1879048192 | bytes 4194304 | tf_op jit(solution)/shard_map/pallas_call | solution.py:457
  67.3 65.2 %shard_map.119 = (bf16[128,2048]{1,0:T(8,128)(2,1)}, bf16[128,2048]{1,0:T(8,128)(2,1)}, bf16[128,2048]{1,0:T(8,128)(2,1)}, bf16[128,2048]{1,0:T(8,128)(2,1)}, f32[16,128]{1,0:T(8,128)}, /*index=5*/f32[16,128]{1,0:T(8,128)}) custom-call(bf16[128,2048]{1,0:T(8,128)(2,1)} %get-tuple-element.18.refs_0_, bf16[128,2048]{1,0:T(8,128)(2,1)} %get-tuple-element.19.refs_1_, ...), custom_call_target="tpu_custom_call" | custom-call | tf_op jit(solution)/shard_map/pallas_call | solution.py:522

commit v4 on v3

--- a/solution.py
+++ b/solution.py
@@ -424,17 +424,22 @@
         store.wait()
 
 
-def writer(*refs):
-    *arrays, sems = refs
-    half = len(arrays) // 2
-    copies = [
-        pltpu.make_async_copy(source, target, sems.at[number])
-        for number, (source, target) in enumerate(zip(arrays[:half], arrays[half:]))
+def writer(count, *refs):
+    sources, targets, between, sems = refs[:count], refs[count : 2 * count], refs[2 * count : -1], refs[-1]
+    steps = [
+        (
+            pltpu.make_async_copy(sources[number], between[number], sems.at[0, number]),
+            pltpu.make_async_copy(between[number], targets[number], sems.at[1, number]),
+        )
+        for number in range(count)
     ]
-    for copy in copies:
-        copy.start()
-    for copy in copies:
-        copy.wait()
+    for load, _ in steps:
+        load.start()
+    for load, store in steps:
+        load.wait()
+        store.start()
+    for _, store in steps:
+        store.wait()
 
 
 def body(group, chain, split_heads, queries, keys, values, log_decay, agent_ids, norm_gain, out_grad):
@@ -520,11 +525,12 @@
         out_grad,
     )
     outs = pl.pallas_call(
-        writer,
+        functools.partial(writer, len(outs)),
         out_shape=[jax.ShapeDtypeStruct(out.shape, out.dtype) for out in outs],
         in_specs=[pl.BlockSpec(memory_space=pltpu.HBM)] * 6,
         out_specs=[pl.BlockSpec(memory_space=pltpu.HBM)] * 6,
-        scratch_shapes=[pltpu.SemaphoreType.DMA((6,))],
+        scratch_shapes=[pltpu.VMEM(out.shape, out.dtype) for out in outs]
+        + [pltpu.SemaphoreType.DMA((2, len(outs)))],
         compiler_params=pltpu.CompilerParams(vmem_limit_bytes=60 * 2**20),
     )(*outs)
     return (*outs[:5], outs[5].reshape(width))

time: 133 us -> 70 us (0.53)
  Pallas kernels: 132 us -> 69.1 us
    pallas_call x1, Pallas kernels: 65.2 us -> 2.46 us  [body(): pl.pallas_call(functools.partial(writer, len(outs)), out_shape=[jax.Shape...]
where the time goes in v4:
time: 70 us; the launch traced here: 69.8 us
  Pallas kernels  69.1 us (99%)
    pallas_call x1, Pallas kernels, body(): pl.pallas_call(functools.partial(kernel, group, chain, split_heads), out_...  66.7 us
    pallas_call x1, Pallas kernels, body(): pl.pallas_call(functools.partial(writer, len(outs)), out_shape=[jax.Shape...  2.46 us

profile of v4, /device:TPU:0, one launch (start us, length us, event | category | flops | bytes accessed | tf_op | source)
XLA Modules:
  0.0 69.8 jit_solution(14446862172956531924)
XLA Ops:
  0.6 66.7 %shard_map.118 = (bf16[128,2048]{1,0:T(8,128)(2,1)}, bf16[128,2048]{1,0:T(8,128)(2,1)}, bf16[128,2048]{1,0:T(8,128)(2,1)}, bf16[128,2048]{1,0:T(8,128)(2,1)}, f32[16,128]{1,0:T(8,128)}, /*index=5*/f32[16,128]{1,0:T(8,128)}) custom-call(bf16[128,2048]{1,0:T(8,128)(2,1)} %q_from.1, bf16[128,2048]{1,0:T(8,128)(2,1)} %k_from.1, bf16[128,2048]{1,0:T(8,128)(2,1)} %v_from.1, ...), custom_call_target="tpu_custom_call" | custom-call | flops 1879048192 | bytes 4194304 | tf_op jit(solution)/shard_map/pallas_call | solution.py:462
  67.3 2.5 %shard_map.119 = (bf16[128,2048]{1,0:T(8,128)(2,1)}, bf16[128,2048]{1,0:T(8,128)(2,1)}, bf16[128,2048]{1,0:T(8,128)(2,1)}, bf16[128,2048]{1,0:T(8,128)(2,1)}, f32[16,128]{1,0:T(8,128)}, /*index=5*/f32[16,128]{1,0:T(8,128)}) custom-call(bf16[128,2048]{1,0:T(8,128)(2,1)} %get-tuple-element.18.refs_0_, bf16[128,2048]{1,0:T(8,128)(2,1)} %get-tuple-element.19.refs_1_, ...), custom_call_target="tpu_custom_call" | custom-call | tf_op jit(solution)/shard_map/pallas_call | solution.py:527

commit v5 on v4

--- a/solution.py
+++ b/solution.py
@@ -101,17 +101,18 @@
 
     def deal(self, chunk):
         for step in range(1, self.group):
+            if chunk > 0:
+                self.deal_copy(step, chunk - 1).wait_send()
             self.deal_copy(step, chunk).start()
         self.dealt[self.inner, chunk] = self.own[self.inner * self.share + chunk]
 
-    def combine(self, chunk):
+    def total(self, chunk):
         for step in range(1, self.group):
             self.deal_copy(step, chunk).wait_recv()
         order = range(self.group)
         row = pl.ds(self.inner * self.share + chunk, 1)
-        passed, through = None, []
+        passed = None
         for place in reversed(order) if self.back else order:
-            through.append((place, passed))
             factor = self.factors[place, row, :]
             term = self.dealt[place, chunk]
             if passed is None:
@@ -120,26 +121,67 @@
             else:
                 self.given[place, chunk] = total
                 total, passed = total * factor + term, passed * factor
-        if self.chain > 1:
-
-            @pl.when(self.first())
-            def _():
-                self.came[chunk] = jnp.zeros_like(total)
-
-            @pl.when(jnp.logical_not(self.first()))
-            def _():
-                self.chain_copy(chunk).wait_recv()
-
+        self.gone[chunk] = total
+
+    def link(self, chunk):
+        order = range(self.group)
+        row = pl.ds(self.inner * self.share + chunk, 1)
+        passed, through = None, []
+        for place in reversed(order) if self.back else order:
+            through.append((place, passed))
+            factor = self.factors[place, row, :]
+            passed = factor if passed is None else passed * factor
+
+        @pl.when(jnp.logical_not(self.first()))
+        def _():
+            self.chain_copy(chunk).wait_recv()
+            self.gone[chunk] += self.came[chunk] * passed
+
+        @pl.when(jnp.logical_not(self.last()))
+        def _():
+            self.chain_copy(chunk).start()
+
+        @pl.when(jnp.logical_not(self.first()))
+        def _():
             before = self.came[chunk]
-            self.gone[chunk] = before * passed + total
-
-            @pl.when(jnp.logical_not(self.last()))
-            def _():
-                self.chain_copy(chunk).start()
-
             for place, factor in through:
                 added = before if factor is None else before * factor
                 self.given[place, chunk] += added
+
+    def run(self, make, between):
+        share, last = self.share, self.share - 1
+        distance = self.chain - 1 - self.outer if self.back else self.outer
+        for chunk in range(min(2, share)):
+            make(chunk)
+            self.deal(chunk)
+        for chunk in range(2, share):
+            make(chunk)
+        early = share - 2
+        for slot in range(early):
+            self.total(slot)
+            if self.chain > 1:
+                for chunk in range(slot + 1):
+
+                    @pl.when(distance == slot - chunk)
+                    def _():
+                        self.link(chunk)
+
+            self.deal(slot + 2)
+        for step in range(1, self.group):
+            self.deal_copy(step, last).wait_send()
+        for chunk in range(share):
+            if chunk >= early:
+                self.total(chunk)
+            if self.chain > 1:
+
+                @pl.when(distance > early - 1 - chunk)
+                def _():
+                    self.link(chunk)
+
+            self.give(chunk)
+            between(chunk)
+
+    def give(self, chunk):
         for step in range(1, self.group):
             self.give_copy(step, chunk).start()
         self.got[self.inner * self.share + chunk] = self.given[self.inner, chunk]
@@ -151,7 +193,6 @@
     def finish(self):
         for chunk in range(self.share):
             for step in range(1, self.group):
-                self.deal_copy(step, chunk).wait_send()
                 self.give_copy(step, chunk).wait_send()
             if self.chain > 1:
 
@@ -275,21 +316,25 @@
 
     for load in loads[1:3]:
         load.wait()
-    each_head(0, own_end)
-    pl.semaphore_wait(barrier, len(inner_peers) + len(outer_peers) + len(side_peers))
     factor_copies = to_peers(factor_ref, inner, inner_peers, "tm", factor_sems)
-    for copy in factor_copies:
-        copy.start()
-    forward.deal(0)
-    for chunk in range(1, share):
+
+    def make_ends(chunk):
         each_head(chunk, own_end)
-        forward.deal(chunk)
-
-    for load in loads[3:]:
-        load.wait()
-    teams = jnp.broadcast_to(lax.div(agent_ref[...], TEAM).astype(F32), (length, length))
-    visible = (rows_at >= lanes_at) & (teams == teams.T)
-    bias_ref[...] = jnp.where(visible, 0.0, -1e30)
+        if chunk == 0:
+            pl.semaphore_wait(barrier, len(inner_peers) + len(outer_peers) + len(side_peers))
+            for copy in factor_copies:
+                copy.start()
+        if chunk == share - 1:
+            for load in loads[3:]:
+                load.wait()
+            make_bias()
+            for copy in factor_copies:
+                copy.wait_recv()
+
+    def make_bias():
+        teams = jnp.broadcast_to(lax.div(agent_ref[...], TEAM).astype(F32), (length, length))
+        visible = (rows_at >= lanes_at) & (teams == teams.T)
+        bias_ref[...] = jnp.where(visible, 0.0, -1e30)
 
     def own_out(head):
         across = sum_ref[row(head), :]
@@ -299,11 +344,7 @@
         score_ref[head] = score
         out_ref[head] = product(split(score), (v_ref[:, columns(head)],), NN)
 
-    for copy in factor_copies:
-        copy.wait_recv()
-    for chunk in range(share):
-        forward.combine(chunk)
-        each_head(chunk, own_out)
+    forward.run(make_ends, lambda chunk: each_head(chunk, own_out))
 
     norm_ref[side] = jnp.zeros_like(norm_ref[side])
 
@@ -339,22 +380,13 @@
         weighted = adjoint * jnp.exp(spread_ref[head]) * scale
         start_ref[head] = product((q_ref[:, columns(head)],), split(weighted), TN)
 
-    for chunk in range(share):
-        each_head(chunk, own_start)
-        backward.deal(chunk)
-
     def result(head):
         normed = out_ref[head] * scale_ref[0]
         y_ref[:, columns(head)] = (normed * gain_ref[row(head), :]).astype(BF16)
         grads = grad_ref[:, columns(head)].astype(F32)
         gain_ref_in[inner, row(head), :] = jnp.sum(grads * normed, axis=0, keepdims=True)
 
-    for chunk in range(share):
-        each_head(chunk, result)
-    stores[0].start()
     gain_copies_in = to_peers(gain_ref_in, inner, inner_peers, "tm", gain_sems_in)
-    for copy in gain_copies_in:
-        copy.start()
 
     def own_grads(head):
         queries, keys = q_ref[:, columns(head)], k_ref[:, columns(head)]
@@ -366,9 +398,14 @@
         k_part_ref[head] = product(pairs, (queries,), TN) * scale
         v_part_ref[head] = product(split(score_ref[head]), adjoint, TN)
 
-    for chunk in range(share):
-        backward.combine(chunk)
+    def beside(chunk):
+        each_head(chunk, result)
         each_head(chunk, own_grads)
+
+    backward.run(lambda chunk: each_head(chunk, own_start), beside)
+    stores[0].start()
+    for copy in gain_copies_in:
+        copy.start()
     stores[1].start()
 
     for copy in gain_copies_in:

time: 70 us -> 76.8 us (1.097)
  Pallas kernels: 69.1 us -> 76 us
    pallas_call x1, Pallas kernels: 66.7 us -> 73.5 us  [body(): pl.pallas_call(functools.partial(kernel, group, chain, split_heads), out_...]
where the time goes in v5:
time: 76.8 us; the launch traced here: 76.6 us
  Pallas kernels  76 us (99%)
    pallas_call x1, Pallas kernels, body(): pl.pallas_call(functools.partial(kernel, group, chain, split_heads), out_...  73.5 us
    pallas_call x1, Pallas kernels, body(): pl.pallas_call(functools.partial(writer, len(outs)), out_shape=[jax.Shape...  2.46 us

profile of v5, /device:TPU:0, one launch (start us, length us, event | category | flops | bytes accessed | tf_op | source)
XLA Modules:
  0.0 76.6 jit_solution(434409212749703977)
XLA Ops:
  0.6 73.5 %shard_map.118 = (bf16[128,2048]{1,0:T(8,128)(2,1)}, bf16[128,2048]{1,0:T(8,128)(2,1)}, bf16[128,2048]{1,0:T(8,128)(2,1)}, bf16[128,2048]{1,0:T(8,128)(2,1)}, f32[16,128]{1,0:T(8,128)}, /*index=5*/f32[16,128]{1,0:T(8,128)}) custom-call(bf16[128,2048]{1,0:T(8,128)(2,1)} %q_from.1, bf16[128,2048]{1,0:T(8,128)(2,1)} %k_from.1, bf16[128,2048]{1,0:T(8,128)(2,1)} %v_from.1, ...), custom_call_target="tpu_custom_call" | custom-call | flops 1879048192 | bytes 4194304 | tf_op jit(solution)/shard_map/pallas_call | solution.py:499
  74.2 2.5 %shard_map.119 = (bf16[128,2048]{1,0:T(8,128)(2,1)}, bf16[128,2048]{1,0:T(8,128)(2,1)}, bf16[128,2048]{1,0:T(8,128)(2,1)}, bf16[128,2048]{1,0:T(8,128)(2,1)}, f32[16,128]{1,0:T(8,128)}, /*index=5*/f32[16,128]{1,0:T(8,128)}) custom-call(bf16[128,2048]{1,0:T(8,128)(2,1)} %get-tuple-element.18.refs_0_, bf16[128,2048]{1,0:T(8,128)(2,1)} %get-tuple-element.19.refs_1_, ...), custom_call_target="tpu_custom_call" | custom-call | tf_op jit(solution)/shard_map/pallas_call | solution.py:564
